TPU v7x, 512 devices: a whole 4x4x16 slice. The times are simulated.
512 devices in a mesh: grp: 8 (over y, core), leaf: 64 (over x, z).
Axes of the slice: x: 4, y: 4, z: 16, core: 2. Of those that a mesh axis runs over, the one named last changes fastest.
Arguments:
- vectors: float32 [16, 524288], P(None, ('grp', 'leaf')), may hold values from -6 to 6
- points: float32 [3, 524288], P(None, ('grp', 'leaf')), may hold values from -1 to 2
- near_lists: int32 [1024, 6], P(('grp', 'leaf')), may hold values from -1 to 5, as said below
- inter_lists: int32 [1024, 16], P(('grp', 'leaf')), may hold values from 0 to 127, as said below
- skeleton: int32 [1024, 64], P(('grp', 'leaf')), may hold values from 0 to 511, as said below
- interp: float32 [1024, 64, 512], P(('grp', 'leaf')), may hold values from -0.25 to 0.25
- transfer: float32 [1024, 64, 128], P(('grp', 'leaf')), may hold values from -0.125 to 0.125
- coarse_points: float32 [8, 3, 128], replicated, may hold values from 0 to 1
Outputs:
- filtered: float32 [16, 524288], P(None, ('grp', 'leaf'))
Inputs may be any that keep to these rules, and one draw needn't show every extreme that they name: `near_lists`: place w of leaf l's window is leaf (l // 2 - 1) * 2 + w. Slot 0 holds the leaf itself (2 + l % 2); the next slots hold distinct places of other leaves of the same subtree; then -1 to the end of the row. `inter_lists`: distinct leaves of the leaf's own subtree, numbered from the subtree's first leaf, none in the leaf's window. `skeleton`: distinct places within the leaf.
All inputs are finite; a program needn't handle non-finite values.
Results may differ from a plain program's by a relative error of at most 0.00013.
Values sent between devices are 32-bit elements; how exact they have to be, the bound alone decides.
A program may use at most 64 MiB of HBM per device.

v0:
```python
import functools

import jax
import jax.numpy as jnp
from jax import lax
from jax.sharding import Mesh
from jax.sharding import PartitionSpec as P

GRP = ("grp_0", "grp_1")
LEAF = ("leaf_0", "leaf_1")
GRP_LEAF = ("grp_0", "grp_1", "leaf_0", "leaf_1")


kappa_scale = 3.4641016151377544
centre = 0.05
half_width = 0.05
highest = lax.Precision.HIGHEST


def laid_out(tiles, dim):
    tiles = jnp.moveaxis(tiles, 0, dim)
    lengths = tiles.shape
    return tiles.reshape(*lengths[:dim], lengths[dim] * lengths[dim + 1], *lengths[dim + 2 :])


def from_everyone(x, axis):
    copies = jnp.broadcast_to(x, (lax.axis_size(axis), *x.shape))
    return lax.all_to_all(copies, axis, split_axis=0, concat_axis=0, tiled=True)


def collect(x, axis, dim):
    return laid_out(from_everyone(x, axis), dim)


def with_halo(x, sides, width):
    for axis, dim in sides:
        devices, length = (lax.axis_size(axis), x.shape[dim])
        up = [(i, (i + 1) % devices) for i in range(devices - 1)]
        down = [(j, i) for i, j in up]
        last = lax.slice_in_dim(x, length - width, length, axis=dim)
        initial = lax.slice_in_dim(x, 0, width, axis=dim)
        before = lax.ppermute(last, axis, up)
        after = lax.ppermute(initial, axis, down)
        x = jnp.concatenate([before, x, after], axis=dim)
    return x


def of_everyone(x, axis):
    return from_everyone(x, axis).sum(axis=0)


def over_axes(x, axes):
    return functools.reduce(lax.psum, axes, x)


def matern(source, target):
    delta_x = source[..., 0, :, None] - target[..., 0, None, :]
    delta_y = source[..., 1, :, None] - target[..., 1, None, :]
    delta_z = source[..., 2, :, None] - target[..., 2, None, :]
    scaled = kappa_scale * jnp.sqrt(delta_x * delta_x + delta_y * delta_y + delta_z * delta_z)
    return (1.0 + scaled) * jnp.exp(-scaled)


def on_device(vectors, points, near_lists, inter_lists, skeleton, interp, transfer, coarse_points):
    per_dev = near_lists.shape[0]
    slot_count = near_lists.shape[1]
    leaf_size = interp.shape[2]
    vec_count = vectors.shape[0]
    group_index = lax.axis_index(GRP)
    group_count = lax.axis_size(GRP)
    leaf_points = points.reshape(3, per_dev, leaf_size).transpose(1, 0, 2)
    skel_points = jnp.take_along_axis(leaf_points, skeleton[:, None, :], axis=2)
    subtree_skel = collect(skel_points, LEAF, 0)
    own_coarse = lax.dynamic_index_in_dim(coarse_points, group_index, 0, keepdims=False)
    apart = (jnp.arange(group_count) != group_index).astype(jnp.float32)
    coupling = matern(coarse_points, own_coarse[None]) * apart[:, None, None]
    live_slots = jnp.max(jnp.sum((near_lists >= 0).astype(jnp.int32), axis=1))
    listed_points = jnp.take(subtree_skel, inter_lists, axis=0)
    far_kernel = matern(listed_points, skel_points[:, None])

    def operate(field):
        stacked = jnp.concatenate([points, field], axis=0)
        window = with_halo(stacked, ((LEAF, 1),), per_dev * leaf_size)
        window_points = window[:3].reshape(3, 3 * per_dev, leaf_size)
        window_vecs = window[3:].reshape(vec_count, 3 * per_dev, leaf_size)

        def near_slot(slot, running):
            chosen = lax.dynamic_index_in_dim(near_lists, slot, 1, keepdims=False)
            present = (chosen >= 0).astype(jnp.float32)
            safe_place = jnp.where(chosen >= 0, chosen, 0)
            source_points = jnp.take(window_points, safe_place, axis=1).transpose(1, 0, 2)
            source_vecs = jnp.take(window_vecs, safe_place, axis=1)
            kernel = matern(source_points, leaf_points)
            product = jnp.einsum("vlp,lpq->lvq", source_vecs, kernel, precision=highest)
            return running + present[:, None, None] * product

        near_part = lax.fori_loop(
            0, live_slots, near_slot, jnp.zeros((per_dev, vec_count, leaf_size), jnp.float32)
        )
        leaf_vecs = field.reshape(vec_count, per_dev, leaf_size)
        coeffs = jnp.einsum("vlp,lrp->lvr", leaf_vecs, interp, precision=highest)
        piece = collect(coeffs, LEAF, 0)
        count = piece.shape[0]
        inside = (inter_lists >= 0) & (inter_lists < count)
        safe_local = jnp.clip(inter_lists, 0, count - 1)
        picked = jnp.take(piece, safe_local, axis=0)
        listed_coeffs = jnp.where(inside[:, :, None, None], picked, 0.0)
        leaf_far = jnp.einsum("lsvr,lsrq->lvq", listed_coeffs, far_kernel, precision=highest)
        upward = jnp.einsum("lvr,lrc->vc", coeffs, transfer, precision=highest)
        subtree_total = of_everyone(upward, LEAF)
        group_coeffs = collect(subtree_total[None], GRP, 0)
        coarse_field = jnp.einsum("avr,arq->vq", group_coeffs, coupling, precision=highest)
        downward = leaf_far + jnp.einsum("vc,lrc->lvr", coarse_field, transfer, precision=highest)
        far_part = jnp.einsum("lvr,lrp->lvp", downward, interp, precision=highest)
        combined = (near_part + far_part) / (leaf_size * slot_count)
        return combined.transpose(1, 0, 2).reshape(vec_count, per_dev * leaf_size)

    term_one = (operate(vectors) - centre * vectors) / half_width
    term_two = 2.0 * (operate(term_one) - centre * term_one) / half_width - vectors
    term_three = 2.0 * (operate(term_two) - centre * term_two) / half_width - term_one
    squares = over_axes(jnp.sum(term_three * term_three, axis=1), GRP_LEAF)
    total_points = vectors.shape[1] * group_count * lax.axis_size(LEAF)
    return term_three / jnp.sqrt(squares / total_points + 1e-06)[:, None]


def solution(mesh):
    torus = Mesh(mesh.devices.reshape(4, 2, 4, 16), ("grp_0", "grp_1", "leaf_0", "leaf_1"))
    in_specs = (
        P(None, GRP_LEAF),
        P(None, GRP_LEAF),
        P(GRP_LEAF, None),
        P(GRP_LEAF, None),
        P(GRP_LEAF, None),
        P(GRP_LEAF, None, None),
        P(GRP_LEAF, None, None),
        P(),
    )
    out_specs = P(None, GRP_LEAF)
    return jax.shard_map(
        on_device, mesh=torus, in_specs=in_specs, out_specs=out_specs, check_vma=False
    )
```

profile of v0, /device:TPU:32, one launch (start us, length us, event | category | flops | bytes accessed | tf_op | source)
XLA Modules:
  0.0 379.5 jit_solution(17428093245418781665)
XLA Ops:
  4.7 18.2 %all-to-all-start.1 = ((f32[64,1,384]{2,1,0:T(1,128)}), f32[64,1,384]{2,1,0:T(1,128)S(1)}, u32[]{:S(2)}, u32[]{:S(2)}) async-start(f32[64,1,384]{2,1,0:T(1,128)} %reshape.309), calls=%async_computation.1 | async-start | bytes 196608 | tf_op jit(solution)/shard_map/all_to_all | solution.py:28
  23.5 14.2 %all-to-all-done.1 = f32[64,1,384]{2,1,0:T(1,128)S(1)} async-done(((f32[64,1,384]{2,1,0:T(1,128)}), f32[64,1,384]{2,1,0:T(1,128)S(1)}, u32[]{:S(2)}, u32[]{:S(2)}) %all-to-all-start.1) | async-done | bytes 98336 | tf_op jit(solution)/shard_map/all_to_all | solution.py:28
  38.5 5.8 %all-to-all-start.2 = ((f32[64,16,128]{2,1,0:T(8,128)}), f32[64,16,128]{2,1,0:T(8,128)S(1)}, u32[]{:S(2)}, u32[]{:S(2)}) async-start(f32[64,16,128]{2,1,0:T(8,128)} %broadcast_in_dim.130), calls=%async_computation.2 | async-start | bytes 1048576 | tf_op jit(solution)/shard_map/all_to_all | solution.py:28
  46.7 3.5 collective-permute-start
  53.2 15.2 %collective-permute-done.1 = f32[19,1024]{1,0:T(8,128)S(1)} collective-permute-done((f32[19,1024]{1,0:T(8,128)S(1)}, f32[19,1024]{1,0:T(8,128)S(1)}, u32[]{:S(2)}, u32[]{:S(2)}) %collective-permute-start.1) | collective-permute-done | bytes 77856 | tf_op jit(solution)/shard_map/ppermute | solution.py:43
  68.5 6.6 %all-to-all-done.2 = f32[64,16,128]{2,1,0:T(8,128)S(1)} async-done(((f32[64,16,128]{2,1,0:T(8,128)}), f32[64,16,128]{2,1,0:T(8,128)S(1)}, u32[]{:S(2)}, u32[]{:S(2)}) %all-to-all-start.2) | async-done | bytes 524320 | tf_op jit(solution)/shard_map/all_to_all | solution.py:28
  75.1 9.2 %all-to-all-start = ((f32[64,1,2048]{2,1,0:T(1,128)}), f32[64,1,2048]{2,1,0:T(1,128)S(1)}, u32[]{:S(2)}, u32[]{:S(2)}) async-start(f32[64,1,2048]{2,1,0:T(1,128)} %reshape.311), calls=%async_computation | async-start | bytes 1048576 | tf_op jit(solution)/shard_map/all_to_all | solution.py:28
  84.3 29.4 %while.30 = (s32[]{:T(128)}, f32[2,16,512]{2,1,0:T(8,128)S(1)}, s32[]{:T(128)}, s32[2,6]{0,1:T(8,128)S(1)}, f32[16,6,512]{2,0,1:T(8,128)S(1)}, /*index=5*/f32[3,...) while((s32[]{:T(128)}, f32[2,16,512]{2,1,0:T(8,128)S(1)}, s32[]{:T(128)}, ...), condition=%wide.region_3.6_spmd, body=%wide.region_2.0_spmd.sunk | while | flops 107008024 | bytes 479441 | solution.py:97
  116.9 4.5 %all-to-all-start.3 = ((f32[8,1,16,128]{3,2,1,0:T(8,128)}), f32[8,1,16,128]{3,2,1,0:T(8,128)S(1)}, u32[]{:S(2)}, u32[]{:S(2)}) async-start(f32[8,1,16,128]{3,2,1,0:T(8,128)} %broadcast_in_dim.131), calls=%async_computation.3 | async-start | bytes 131072 | tf_op jit(solution)/shard_map/all_to_all | solution.py:28
  129.8 15.1 %all-to-all-start.5 = ((f32[64,16,128]{2,1,0:T(8,128)}), f32[64,16,128]{2,1,0:T(8,128)S(1)}, u32[]{:S(2)}, u32[]{:S(2)}) async-start(f32[64,16,128]{2,1,0:T(8,128)} %broadcast_in_dim.133), calls=%async_computation.5 | async-start | bytes 1048576 | tf_op jit(solution)/shard_map/all_to_all | solution.py:28
  152.4 17.2 %collective-permute-done.3 = f32[19,1024]{1,0:T(8,128)S(1)} collective-permute-done((f32[19,1024]{1,0:T(8,128)S(1)}, f32[19,1024]{1,0:T(8,128)S(1)}, u32[]{:S(2)}, u32[]{:S(2)}) %collective-permute-start.3) | collective-permute-done | bytes 77856 | tf_op jit(solution)/shard_map/ppermute | solution.py:43
  169.7 6.6 %all-to-all-done.5 = f32[64,16,128]{2,1,0:T(8,128)S(1)} async-done(((f32[64,16,128]{2,1,0:T(8,128)}), f32[64,16,128]{2,1,0:T(8,128)S(1)}, u32[]{:S(2)}, u32[]{:S(2)}) %all-to-all-start.5) | async-done | bytes 524320 | tf_op jit(solution)/shard_map/all_to_all | solution.py:28
  176.3 9.1 %all-to-all-start.4 = ((f32[64,1,2048]{2,1,0:T(1,128)}), f32[64,1,2048]{2,1,0:T(1,128)S(1)}, u32[]{:S(2)}, u32[]{:S(2)}) async-start(f32[64,1,2048]{2,1,0:T(1,128)} %reshape.313), calls=%async_computation.4 | async-start | bytes 1048576 | tf_op jit(solution)/shard_map/all_to_all | solution.py:28
  185.4 29.4 %while.31 = (s32[]{:T(128)}, f32[2,16,512]{2,1,0:T(8,128)S(1)}, s32[]{:T(128)}, s32[2,6]{0,1:T(8,128)S(1)}, f32[16,6,512]{2,0,1:T(8,128)S(1)}, /*index=5*/f32[3,...) while((s32[]{:T(128)}, f32[2,16,512]{2,1,0:T(8,128)S(1)}, s32[]{:T(128)}, ...), condition=%wide.region_6.10_spmd, body=%wide.region_5.9_spmd.sunk | while | flops 107008024 | bytes 479441 | solution.py:97
  216.9 4.6 %all-to-all-start.6 = ((f32[8,1,16,128]{3,2,1,0:T(8,128)}), f32[8,1,16,128]{3,2,1,0:T(8,128)S(1)}, u32[]{:S(2)}, u32[]{:S(2)}) async-start(f32[8,1,16,128]{3,2,1,0:T(8,128)} %broadcast_in_dim.134), calls=%async_computation.6 | async-start | bytes 131072 | tf_op jit(solution)/shard_map/all_to_all | solution.py:28
  229.9 13.5 %all-to-all-start.8 = ((f32[64,16,128]{2,1,0:T(8,128)}), f32[64,16,128]{2,1,0:T(8,128)S(1)}, u32[]{:S(2)}, u32[]{:S(2)}) async-start(f32[64,16,128]{2,1,0:T(8,128)} %broadcast_in_dim.136), calls=%async_computation.8 | async-start | bytes 1048576 | tf_op jit(solution)/shard_map/all_to_all | solution.py:28
  250.9 17.2 %collective-permute-done.5 = f32[19,1024]{1,0:T(8,128)S(1)} collective-permute-done((f32[19,1024]{1,0:T(8,128)S(1)}, f32[19,1024]{1,0:T(8,128)S(1)}, u32[]{:S(2)}, u32[]{:S(2)}) %collective-permute-start.5) | collective-permute-done | bytes 77856 | tf_op jit(solution)/shard_map/ppermute | solution.py:43
  268.1 6.6 %all-to-all-done.8 = f32[64,16,128]{2,1,0:T(8,128)S(1)} async-done(((f32[64,16,128]{2,1,0:T(8,128)}), f32[64,16,128]{2,1,0:T(8,128)S(1)}, u32[]{:S(2)}, u32[]{:S(2)}) %all-to-all-start.8) | async-done | bytes 524320 | tf_op jit(solution)/shard_map/all_to_all | solution.py:28
  274.7 9.1 %all-to-all-start.7 = ((f32[64,1,2048]{2,1,0:T(1,128)}), f32[64,1,2048]{2,1,0:T(1,128)S(1)}, u32[]{:S(2)}, u32[]{:S(2)}) async-start(f32[64,1,2048]{2,1,0:T(1,128)} %reshape.315), calls=%async_computation.7 | async-start | bytes 1048576 | tf_op jit(solution)/shard_map/all_to_all | solution.py:28
  283.8 29.6 %while.32 = (s32[]{:T(128)}, f32[2,16,512]{2,1,0:T(8,128)S(1)}, s32[]{:T(128)}, s32[2,6]{0,1:T(8,128)S(1)}, f32[16,6,512]{2,0,1:T(8,128)S(1)}, /*index=5*/f32[3,...) while((s32[]{:T(128)}, f32[2,16,512]{2,1,0:T(8,128)S(1)}, s32[]{:T(128)}, ...), condition=%wide.region_9.13_spmd, body=%wide.region_8.12_spmd.sunk | while | flops 107008024 | bytes 479441 | solution.py:97
  315.3 4.6 %all-to-all-start.9 = ((f32[8,1,16,128]{3,2,1,0:T(8,128)}), f32[8,1,16,128]{3,2,1,0:T(8,128)S(1)}, u32[]{:S(2)}, u32[]{:S(2)}) async-start(f32[8,1,16,128]{3,2,1,0:T(8,128)} %broadcast_in_dim.137), calls=%async_computation.9 | async-start | bytes 131072 | tf_op jit(solution)/shard_map/all_to_all | solution.py:28
  327.1 10.3 %psum.28 = f32[16]{0:T(128)S(1)} all-reduce(f32[16]{0:T(128)S(1)} %multiply_reduce_fusion), channel_id=1, replica_groups=mesh['grp_0'=4,'grp_1'=2,'leaf_0'=4,'leaf_1'=16] {'grp_0'}, use_global_device_ids=true, to_apply=%region_12.16 | all-reduce | flops 16 | bytes 128 | tf_op jit(solution)/shard_map/psum | solution.py:53
  339.8 10.8 %psum.30 = f32[16]{0:T(128)S(1)} all-reduce(f32[16]{0:T(128)S(1)} %psum.29), channel_id=1, replica_groups=mesh['grp_0'=4,'grp_1'=2,'leaf_0'=4,'leaf_1'=16] {'leaf_0'}, use_global_device_ids=true, to_apply=%region_14.18 | all-reduce | flops 16 | bytes 128 | tf_op jit(solution)/shard_map/psum | solution.py:53
  350.6 28.1 %psum.31 = f32[16]{0:T(128)S(1)} all-reduce(f32[16]{0:T(128)S(1)} %psum.30), channel_id=1, replica_groups=mesh['grp_0'=4,'grp_1'=2,'leaf_0'=4,'leaf_1'=16] {'leaf_1'}, use_global_device_ids=true, to_apply=%region_15.19 | all-reduce | flops 16 | bytes 128 | tf_op jit(solution)/shard_map/psum | solution.py:53
  (291 shorter events, 132.9 us)
Async XLA Ops:
  0.0 22.9 %copy-start = (f32[2,64,512]{2,1,0:T(8,128)S(1)}, f32[2,64,512]{2,1,0:T(8,128)}, u32[]{:S(2)}) copy-start(f32[2,64,512]{2,1,0:T(8,128)} %param.25) | copy-start | bytes 786436
  0.0 22.9 %copy-start.2 = (f32[16,1024]{1,0:T(8,128)S(1)}, f32[16,1024]{1,0:T(8,128)}, u32[]{:S(2)}) copy-start(f32[16,1024]{1,0:T(8,128)} %param.20) | copy-start | bytes 196612
  0.0 23.2 %copy-start.1 = (f32[2,64,128]{2,1,0:T(8,128)S(1)}, f32[2,64,128]{2,1,0:T(8,128)}, u32[]{:S(2)}) copy-start(f32[2,64,128]{2,1,0:T(8,128)} %param.26) | copy-start | bytes 196612
  4.7 33.0 %all-to-all-start.1 = ((f32[64,1,384]{2,1,0:T(1,128)}), f32[64,1,384]{2,1,0:T(1,128)S(1)}, u32[]{:S(2)}, u32[]{:S(2)}) async-start(f32[64,1,384]{2,1,0:T(1,128)} %reshape.309), calls=%async_computation.1 | async-start | bytes 196608 | tf_op jit(solution)/shard_map/all_to_all | solution.py:28
  22.9 21.4 %copy-start.3 = (f32[3,1024]{1,0:T(4,128)S(1)}, f32[3,1024]{1,0:T(4,128)}, u32[]{:S(2)}) copy-start(f32[3,1024]{1,0:T(4,128)} %param.21) | copy-start | bytes 36868
  23.5 26.9 %copy-start.5 = (s32[2,16]{1,0:T(2,128)S(1)}, s32[2,16]{1,0:T(2,128)}, u32[]{:S(2)}) copy-start(s32[2,16]{1,0:T(2,128)} %param.23) | copy-start | bytes 388
  23.5 27.1 %copy-start.6 = (s32[2,6]{1,0:T(2,128)S(1)}, s32[2,6]{1,0:T(2,128)}, u32[]{:S(2)}) copy-start(s32[2,6]{1,0:T(2,128)} %param.22) | copy-start | bytes 148
  38.5 36.6 %all-to-all-start.2 = ((f32[64,16,128]{2,1,0:T(8,128)}), f32[64,16,128]{2,1,0:T(8,128)S(1)}, u32[]{:S(2)}, u32[]{:S(2)}) async-start(f32[64,16,128]{2,1,0:T(8,128)} %broadcast_in_dim.130), calls=%async_computation.2 | async-start | bytes 1048576 | tf_op jit(solution)/shard_map/all_to_all | solution.py:28
  44.3 24.0 %collective-permute-start.1 = (f32[19,1024]{1,0:T(8,128)S(1)}, f32[19,1024]{1,0:T(8,128)S(1)}, u32[]{:S(2)}, u32[]{:S(2)}) collective-permute-start(f32[19,1024]{1,0:T(8,128)S(1)} %pad_maximum_fusion.3), channel_id=1, source_target_pairs={{1,0},{2,1},{3,2},{4,3},{5,4},{6,5},{7,6},{8,7},{9,8},{10,9},{11,1... | collective-permute-start | bytes 233480 | tf_op jit(solution)/shard_map/ppermute | solution.py:43
  46.7 21.7 %collective-permute-start = (f32[19,1024]{1,0:T(8,128)S(1)}, f32[19,1024]{1,0:T(8,128)S(1)}, u32[]{:S(2)}, u32[]{:S(2)}) collective-permute-start(f32[19,1024]{1,0:T(8,128)S(1)} %pad_maximum_fusion.3), channel_id=1, source_target_pairs={{0,1},{1,2},{2,3},{3,4},{4,5},{5,6},{6,7},{7,8},{8,9},{9,10},{10,1... | collective-permute-start | bytes 233480 | tf_op jit(solution)/shard_map/ppermute | solution.py:42
  50.8 2.3 copy-start.4
  75.1 41.2 %all-to-all-start = ((f32[64,1,2048]{2,1,0:T(1,128)}), f32[64,1,2048]{2,1,0:T(1,128)S(1)}, u32[]{:S(2)}, u32[]{:S(2)}) async-start(f32[64,1,2048]{2,1,0:T(1,128)} %reshape.311), calls=%async_computation | async-start | bytes 1048576 | tf_op jit(solution)/shard_map/all_to_all | solution.py:28
  116.9 10.1 %all-to-all-start.3 = ((f32[8,1,16,128]{3,2,1,0:T(8,128)}), f32[8,1,16,128]{3,2,1,0:T(8,128)S(1)}, u32[]{:S(2)}, u32[]{:S(2)}) async-start(f32[8,1,16,128]{3,2,1,0:T(8,128)} %broadcast_in_dim.131), calls=%async_computation.3 | async-start | bytes 131072 | tf_op jit(solution)/shard_map/all_to_all | solution.py:28
  129.8 46.5 %all-to-all-start.5 = ((f32[64,16,128]{2,1,0:T(8,128)}), f32[64,16,128]{2,1,0:T(8,128)S(1)}, u32[]{:S(2)}, u32[]{:S(2)}) async-start(f32[64,16,128]{2,1,0:T(8,128)} %broadcast_in_dim.133), calls=%async_computation.5 | async-start | bytes 1048576 | tf_op jit(solution)/shard_map/all_to_all | solution.py:28
  145.0 24.6 %collective-permute-start.3 = (f32[19,1024]{1,0:T(8,128)S(1)}, f32[19,1024]{1,0:T(8,128)S(1)}, u32[]{:S(2)}, u32[]{:S(2)}) collective-permute-start(f32[19,1024]{1,0:T(8,128)S(1)} %pad_maximum_fusion.4), channel_id=1, source_target_pairs={{1,0},{2,1},{3,2},{4,3},{5,4},{6,5},{7,6},{8,7},{9,8},{10,9},{11,1... | collective-permute-start | bytes 233480 | tf_op jit(solution)/shard_map/ppermute | solution.py:43
  147.4 22.3 %collective-permute-start.2 = (f32[19,1024]{1,0:T(8,128)S(1)}, f32[19,1024]{1,0:T(8,128)S(1)}, u32[]{:S(2)}, u32[]{:S(2)}) collective-permute-start(f32[19,1024]{1,0:T(8,128)S(1)} %pad_maximum_fusion.4), channel_id=1, source_target_pairs={{0,1},{1,2},{2,3},{3,4},{4,5},{5,6},{6,7},{7,8},{8,9},{9,10},{10,1... | collective-permute-start | bytes 233480 | tf_op jit(solution)/shard_map/ppermute | solution.py:42
  176.3 40.0 %all-to-all-start.4 = ((f32[64,1,2048]{2,1,0:T(1,128)}), f32[64,1,2048]{2,1,0:T(1,128)S(1)}, u32[]{:S(2)}, u32[]{:S(2)}) async-start(f32[64,1,2048]{2,1,0:T(1,128)} %reshape.313), calls=%async_computation.4 | async-start | bytes 1048576 | tf_op jit(solution)/shard_map/all_to_all | solution.py:28
  216.9 10.2 %all-to-all-start.6 = ((f32[8,1,16,128]{3,2,1,0:T(8,128)}), f32[8,1,16,128]{3,2,1,0:T(8,128)S(1)}, u32[]{:S(2)}, u32[]{:S(2)}) async-start(f32[8,1,16,128]{3,2,1,0:T(8,128)} %broadcast_in_dim.134), calls=%async_computation.6 | async-start | bytes 131072 | tf_op jit(solution)/shard_map/all_to_all | solution.py:28
  229.9 44.8 %all-to-all-start.8 = ((f32[64,16,128]{2,1,0:T(8,128)}), f32[64,16,128]{2,1,0:T(8,128)S(1)}, u32[]{:S(2)}, u32[]{:S(2)}) async-start(f32[64,16,128]{2,1,0:T(8,128)} %broadcast_in_dim.136), calls=%async_computation.8 | async-start | bytes 1048576 | tf_op jit(solution)/shard_map/all_to_all | solution.py:28
  243.4 24.6 %collective-permute-start.5 = (f32[19,1024]{1,0:T(8,128)S(1)}, f32[19,1024]{1,0:T(8,128)S(1)}, u32[]{:S(2)}, u32[]{:S(2)}) collective-permute-start(f32[19,1024]{1,0:T(8,128)S(1)} %pad_maximum_fusion.5), channel_id=1, source_target_pairs={{1,0},{2,1},{3,2},{4,3},{5,4},{6,5},{7,6},{8,7},{9,8},{10,9},{11,1... | collective-permute-start | bytes 233480 | tf_op jit(solution)/shard_map/ppermute | solution.py:43
  245.8 22.3 %collective-permute-start.4 = (f32[19,1024]{1,0:T(8,128)S(1)}, f32[19,1024]{1,0:T(8,128)S(1)}, u32[]{:S(2)}, u32[]{:S(2)}) collective-permute-start(f32[19,1024]{1,0:T(8,128)S(1)} %pad_maximum_fusion.5), channel_id=1, source_target_pairs={{0,1},{1,2},{2,3},{3,4},{4,5},{5,6},{6,7},{7,8},{8,9},{9,10},{10,1... | collective-permute-start | bytes 233480 | tf_op jit(solution)/shard_map/ppermute | solution.py:42
  274.7 40.0 %all-to-all-start.7 = ((f32[64,1,2048]{2,1,0:T(1,128)}), f32[64,1,2048]{2,1,0:T(1,128)S(1)}, u32[]{:S(2)}, u32[]{:S(2)}) async-start(f32[64,1,2048]{2,1,0:T(1,128)} %reshape.315), calls=%async_computation.7 | async-start | bytes 1048576 | tf_op jit(solution)/shard_map/all_to_all | solution.py:28
  315.3 10.2 %all-to-all-start.9 = ((f32[8,1,16,128]{3,2,1,0:T(8,128)}), f32[8,1,16,128]{3,2,1,0:T(8,128)S(1)}, u32[]{:S(2)}, u32[]{:S(2)}) async-start(f32[8,1,16,128]{3,2,1,0:T(8,128)} %broadcast_in_dim.137), calls=%async_computation.9 | async-start | bytes 131072 | tf_op jit(solution)/shard_map/all_to_all | solution.py:28
where the time goes:
time: 381 us; the launch traced here: 379 us
  starting transfers between devices  111 us (29%)
  waiting for transfers between devices  88 us (23%)
  matrix products  62.1 us (16%)
  blocking collectives  51.7 us (14%)
  local copies, waits for them, and re-layouts  38.3 us (10%)
  loops' own time  16.2 us (4%)
  other arithmetic  11.5 us (3%)
    all_to_all x10, starting transfers between devices, from_everyone(): return lax.all_to_all(copies, axis, split_axis=0, concat_axis=0, tiled=True)  93.5 us
    psum x4, blocking collectives, over_axes(): return functools.reduce(lax.psum, axes, x)  51.7 us
    dot_general x18, matrix products, near_slot(): product = jnp.einsum('vlp,lpq->lvq', source_vecs, kernel, precision=highest)  50 us
    ppermute x3, waiting for transfers between devices, with_halo(): after = lax.ppermute(initial, axis, down)  49.5 us
    all_to_all x10, waiting for transfers between devices, from_everyone(): return lax.all_to_all(copies, axis, split_axis=0, concat_axis=0, tiled=True)  38.4 us
    another operation x3, loops' own time, operate(): lax.fori_loop(0, live_slots, near_slot, jnp.zeros((per_dev, vec_count, le...  16.2 us
    ppermute x3, starting transfers between devices, with_halo(): before = lax.ppermute(last, axis, up)  10.4 us
    gather x18, local copies, waits for them, and re-layouts, near_slot(): jnp.take(window_points, safe_place, axis=1).transpose(1, 0, 2)  10.3 us
  transfers between devices with their start and end apart: 16, of which 12 were waited for; matrix products, arithmetic and copies ran while one was open for 25% of the time, Pallas kernels for 0%

commit v1 on v0

v1 whole, which is shorter than its diff:
```python
import jax
import jax.numpy as jnp
from jax import lax
from jax.experimental import pallas as pl
from jax.experimental.pallas import tpu as pltpu
from jax.sharding import PartitionSpec as P

MESH = pl.DeviceIdType.MESH
F32, BF16 = jnp.float32, jnp.bfloat16
LN2 = 0.6931471805599453
ALPHA = 3.4641016151377544 / LN2
FAR_AWAY = 65536.0
CENTRE = 0.05
HALF_WIDTH = 0.05
POINTS = 524288
SCALE = 3072.0
PTS, SRC, TGT, HALO, CO, PLANE, ZED, EX, FAR, NORM_P, NORM_Z = 0, 1, 2, 3, 6, 9, 12, 15, 18, 21, 22
SEMS = 23


def dot(a, b):
    return jnp.dot(a, b, preferred_element_type=F32)


def split2(v):
    hi = v.astype(BF16)
    return hi, (v - hi.astype(F32)).astype(BF16)


def stacked(v):
    hi = v.astype(BF16).astype(F32)
    return jnp.concatenate([hi, v - hi], axis=0).astype(BF16)


def dot3(v2, whi, wlo):
    a = dot(v2, whi)
    return a[:16] + a[16:] + dot(v2[:16], wlo)


def split3(v):
    h = v.astype(BF16).astype(F32)
    m = (v - h).astype(BF16).astype(F32)
    return h, m, v - h - m


def norm_rows(q):
    h, m, lo = split3(jnp.sum(q * q, axis=0, keepdims=True))
    row = lax.broadcasted_iota(jnp.int32, q.shape, 0)
    parts = jnp.where(row == 0, h, jnp.where(row == 1, m, jnp.where(row == 2, lo, 0.0)))
    return parts, jnp.where(row < 3, 1.0, 0.0)


def source_features(q, mask_rows):
    h, m, lo = split3(q)
    parts, ones = norm_rows(q)
    pad = jnp.zeros((64 - mask_rows.shape[0], q.shape[1]), F32)
    return jnp.concatenate(
        [-2.0 * h, -2.0 * h, -2.0 * m, -2.0 * m, -2.0 * h, -2.0 * lo, parts, ones, mask_rows, pad], axis=0
    )


def target_features(q, mask_rows):
    h, m, lo = split3(q)
    parts, ones = norm_rows(q)
    pad = jnp.zeros((64 - mask_rows.shape[0], q.shape[1]), F32)
    return jnp.concatenate([h, m, h, m, lo, h, ones, parts, mask_rows, pad], axis=0).astype(BF16)


def matern(d):
    t = jnp.maximum(d, 1e-12)
    s = t * lax.rsqrt(t)
    return (1.0 + LN2 * s) * jnp.exp2(-s)


def kernel(
    vec_ref, pts_ref, near_ref, inter_ref, skel_ref, interp_ref, trans_ref, coarse_ref, out_ref,
    xs, xh, vh, ybuf, vcat, nacc, bhi, blo, bthi, btlo, tgt_near, src_f, khi, klo,
    s_send, s_recv, t_send, t_recv, tgt_far, fhi, flo, kc,
    usend, precv, wsend, zrecv, hsend, xrecv, csend, crecv, gsend, grecv,
    nsend, np_recv, nz_send, nz_recv, send_sem, recv_sem,
):
    g = lax.axis_index("grp")
    leaf = lax.axis_index("leaf")
    x, z = leaf // 16, leaf % 16
    zh, zl = z // 2, z % 2
    plane = g * 4 + x
    rho = x * 2 + zl

    def z_peer(k):
        return (g, x * 16 + lax.rem(z + k, 16))

    def plane_index(k):
        return lax.rem(plane + k, 32)

    def plane_peer(k):
        i = plane_index(k)
        return (i // 4, lax.rem(i, 4) * 16 + z)

    def x_peer(k):
        return (g, lax.rem(x + k, 4) * 16 + z)

    def r_peer(k):
        i = lax.rem(rho + k, 8)
        return (g, (i // 2) * 16 + zh * 2 + lax.rem(i, 2))

    def c_peer(k):
        return (g, x * 16 + lax.rem(zh + k, 8) * 2 + zl)

    right, left = (g, lax.rem(leaf + 1, 64)), (g, lax.rem(leaf + 63, 64))

    def send(src, dst, sem, peer):
        pltpu.make_async_remote_copy(
            src_ref=src, dst_ref=dst, send_sem=send_sem.at[sem], recv_sem=recv_sem.at[sem],
            device_id=peer, device_id_type=MESH,
        ).start()

    def arrived(ref, sem):
        pltpu.make_async_copy(ref, ref, recv_sem.at[sem]).wait()

    def sent(ref, sem):
        pltpu.make_async_copy(ref, ref, send_sem.at[sem]).wait()

    barrier = pltpu.get_barrier_semaphore()

    def greet(peer):
        pl.semaphore_signal(barrier, inc=1, device_id=peer, device_id_type=MESH)

    for k in range(1, 16):
        greet(z_peer(k))
    for k in range(1, 32):
        greet(plane_peer(k))
    for k in range(1, 8):
        greet(r_peer(k))
    greet(right)
    greet(left)

    xs[...] = jnp.zeros_like(xs)
    xs[0:3, :] = pts_ref[...]
    origin = xs[:, 0:1]

    for l in range(2):
        t_t = trans_ref[l].T
        e = jnp.dot(t_t, interp_ref[l], precision=lax.Precision.HIGHEST, preferred_element_type=F32)
        zero = jnp.zeros((64, 512), F32)
        lower = [interp_ref[l], zero] if l == 0 else [zero, interp_ref[l]]
        b = jnp.concatenate([e, *lower], axis=0)
        hi, lo = split2(b)
        bhi[:, l * 512 : (l + 1) * 512] = hi
        blo[:, l * 512 : (l + 1) * 512] = lo
        hi, lo = split2(b.T)
        bthi[l * 512 : (l + 1) * 512, :] = hi
        btlo[l * 512 : (l + 1) * 512, :] = lo

    both = []
    for l in range(2):
        pick = lax.broadcasted_iota(jnp.int32, (512, 64), 0) == skel_ref[l : l + 1, :]
        pick = jnp.where(pick, 1.0, 0.0).astype(BF16)
        h, m, lo = split3(xs[:, l * 512 : (l + 1) * 512])
        got = dot(jnp.concatenate([h, m, lo, jnp.zeros_like(h)], axis=0).astype(BF16), pick)
        both.append(got[0:8] + (got[8:16] + got[16:24]))
    skel = jnp.concatenate(both, axis=1)
    s_send[...] = skel
    s_recv[rho] = skel

    row = lax.broadcasted_iota(jnp.int32, (128, 128), 0)
    number = ((row >> 2) & 3) * 32 + (row >> 4) * 4 + (row & 3)
    first = lax.broadcasted_iota(jnp.int32, (1, 128), 1) < 64
    listed = jnp.zeros((128, 128), F32)
    for s in range(16):
        wanted = jnp.where(first, inter_ref[0, s], inter_ref[1, s])
        listed = jnp.where(number == wanted, 1.0, listed)
    off = (1.0 - listed) * FAR_AWAY
    for j in range(8):
        t_send[j, 0:8, :] = skel
        t_send[j, 8:24, :] = off[j * 16 : (j + 1) * 16]
    t_recv[zh] = t_send[zh]

    def split_field(y):
        vcat[:, 1024:2048] = stacked(y)

    def upward(i):
        uc = dot3(vcat[:, 1024:2048], bthi[...], btlo[...])
        for j in range(4):
            usend[i, j] = uc[4 * j : 4 * j + 4, 0:128]
        precv[i, plane] = usend[i, x]
        csend[i] = uc[:, 128:256]
        crecv[i, rho] = uc[:, 128:256]

    def send_plane(i):
        for k in range(1, 32):
            send(usend.at[i, lax.rem(plane_index(k), 4)], precv.at[i, plane], PLANE + i, plane_peer(k))

    def send_coeffs(i):
        for k in range(1, 8):
            send(csend.at[i], crecv.at[i, rho], CO + i, r_peer(k))

    def send_halo(i, field):
        send(field, vh.at[i, 0], HALO + i, right)
        send(field, vh.at[i, 1], HALO + i, left)

    def plane_to_z(i):
        arrived(precv.at[i, pl.ds(0, 31)], PLANE + i)
        cols = []
        for e in range(8):
            cols.append((precv[i, 4 * e] + precv[i, 4 * e + 1]) + (precv[i, 4 * e + 2] + precv[i, 4 * e + 3]))
        c4 = jnp.concatenate(cols, axis=1)
        hi = c4.astype(BF16).astype(F32)
        lhs = jnp.concatenate([hi, c4 - hi, jnp.zeros((8, 1024), F32)], axis=0).astype(BF16)
        r = dot(lhs, kc[...])
        w = r[0:4, 0:128] + r[4:8, 0:128] + r[0:4, 128:256]
        wsend[i] = w
        zrecv[i, z] = w
        for k in range(1, 16):
            send(wsend.at[i], zrecv.at[i, z], ZED + i, z_peer(k))

    def z_to_x(i):
        arrived(zrecv.at[i, pl.ds(0, 15)], ZED + i)
        h = jnp.sum(zrecv[i], axis=0)
        hsend[i] = h
        xrecv[i, x] = h
        for k in range(1, 4):
            send(hsend.at[i], xrecv.at[i, x], EX + i, x_peer(k))

    def far_partial(i):
        arrived(crecv.at[i, pl.ds(0, 7)], CO + i)
        c = jnp.concatenate([crecv[i, j] for j in range(8)], axis=1)
        part = dot3(stacked(c), fhi[...], flo[...])
        for j in range(8):
            gsend[i, j] = part[:, j * 128 : (j + 1) * 128]
        grecv[i, zh] = gsend[i, zh]
        for k in range(1, 8):
            send(gsend.at[i, lax.rem(zh + k, 8)], grecv.at[i, zh], FAR + i, c_peer(k))

    def near(lo, hi):
        return dot3(vcat[:, lo:hi], khi[lo:hi, :], klo[lo:hi, :])

    def take_halo(i):
        arrived(vh.at[i], HALO + i)
        vcat[:, 0:1024] = stacked(vh[i, 0])
        vcat[:, 2048:3072] = stacked(vh[i, 1])

    def downward(i):
        arrived(grecv.at[i, pl.ds(0, 7)], FAR + i)
        gq = jnp.sum(grecv[i], axis=0)
        arrived(xrecv.at[i, pl.ds(0, 3)], EX + i)
        h = jnp.concatenate([xrecv[i, j] for j in range(4)], axis=0)
        return (nacc[...] + dot3(stacked(jnp.concatenate([h, gq], axis=1)), bhi[...], blo[...])) / SCALE

    def local(v):
        return (v - origin) * ALPHA

    def near_features(points, first_place):
        r = lax.broadcasted_iota(jnp.int32, (8, 1024), 0)
        place = first_place + lax.broadcasted_iota(jnp.int32, (8, 1024), 1) // 512
        f = source_features(local(points), jnp.where(r == place, 1.0, 0.0))
        src_f[...] = f.T.astype(BF16)

    def near_kernel(base):
        def body(i, _):
            r = pl.multiple_of(i * 256, 256)
            for c in (0, 512):
                k = matern(dot(src_f[pl.ds(r, 256), :], tgt_near[:, c : c + 512]))
                hi, lo = split2(k)
                khi[pl.ds(base + r, 256), c : c + 512] = hi
                klo[pl.ds(base + r, 256), c : c + 512] = lo
            return 0

        lax.fori_loop(0, 4, body, 0)

    def far_kernel():
        half = lax.broadcasted_iota(jnp.int32, (16, 128), 1) // 64
        r = lax.broadcasted_iota(jnp.int32, (16, 128), 0)
        for j in range(8):
            f = source_features(local(s_recv[j]), jnp.where(r == 2 * j + half, 1.0, 0.0))
            src_f[j * 128 : (j + 1) * 128, :] = f.T.astype(BF16)
            tgt_far[:, j * 128 : (j + 1) * 128] = target_features(local(t_recv[j, 0:8, :]), t_recv[j, 8:24, :])

        def body(i, _):
            r = pl.multiple_of(i * 256, 256)
            for c in (0, 512):
                k = matern(dot(src_f[pl.ds(r, 256), :], tgt_far[:, c : c + 512]))
                hi, lo = split2(k)
                fhi[pl.ds(r, 256), c : c + 512] = hi
                flo[pl.ds(r, 256), c : c + 512] = lo
            return 0

        lax.fori_loop(0, 4, body, 0)

    def coarse_kernel():
        none = jnp.zeros((8, 128), F32)
        pad = jnp.zeros((5, 128), F32)
        own = (jnp.concatenate([coarse_ref[g], pad], axis=0) - 0.5) * ALPHA
        tgt = target_features(own, none)
        for e in range(8):
            q = (jnp.concatenate([coarse_ref[e], pad], axis=0) - 0.5) * ALPHA
            k = matern(dot(source_features(q, none).T.astype(BF16), tgt))
            k = k * jnp.where(g == e, 0.0, 1.0)
            hi, lo = split2(k)
            kc[e * 128 : (e + 1) * 128, 0:128] = hi
            kc[e * 128 : (e + 1) * 128, 128:256] = lo

    split_field(vec_ref[...])
    upward(0)

    pl.semaphore_wait(barrier, 15 + 31 + 7 + 2)

    send_plane(0)
    for k in range(1, 8):
        send(t_send.at[lax.rem(zh + k, 8)], t_recv.at[zh], TGT, c_peer(k))
    for k in range(1, 8):
        send(s_send, s_recv.at[rho], SRC, r_peer(k))
    send_coeffs(0)
    send(xs, xh.at[0], PTS, right)
    send(xs, xh.at[1], PTS, left)
    send_halo(0, vec_ref)

    coarse_kernel()
    r = lax.broadcasted_iota(jnp.int32, (8, 1024), 0)
    first = lax.broadcasted_iota(jnp.int32, (1, 1024), 1) < 512
    listed = jnp.zeros((8, 1024), F32)
    for s in range(6):
        listed = jnp.where(r == jnp.where(first, near_ref[0, s], near_ref[1, s]), 1.0, listed)
    tgt_near[...] = target_features(local(xs[...]), (1.0 - listed) * FAR_AWAY)
    near_features(xs[...], 2)
    near_kernel(1024)
    plane_to_z(0)
    nacc[...] = near(1024, 2048)
    arrived(s_recv.at[pl.ds(0, 7)], SRC)
    arrived(t_recv.at[pl.ds(0, 7)], TGT)
    far_kernel()
    far_partial(0)
    arrived(xh, PTS)
    near_features(xh[0], 0)
    near_kernel(0)
    z_to_x(0)
    near_features(xh[1], 4)
    near_kernel(2048)
    take_halo(0)
    nacc[...] += near(0, 1024) + near(2048, 3072)
    y = (downward(0) - CENTRE * vec_ref[...]) / HALF_WIDTH
    ybuf[0] = y

    for i in (1, 2):
        split_field(ybuf[i - 1])
        upward(i)
        send_plane(i)
        send_coeffs(i)
        send_halo(i, ybuf.at[i - 1])
        nacc[...] = near(1024, 2048)
        far_partial(i)
        plane_to_z(i)
        take_halo(i)
        nacc[...] += near(0, 1024) + near(2048, 3072)
        z_to_x(i)
        before = vec_ref[...] if i == 1 else ybuf[0]
        y = 2.0 * (downward(i) - CENTRE * ybuf[i - 1]) / HALF_WIDTH - before
        if i == 1:
            ybuf[1] = y

    lane = lax.broadcasted_iota(jnp.int32, (16, 128), 1)
    diagonal = lane == lax.broadcasted_iota(jnp.int32, (16, 128), 0)
    squares = jnp.sum(y * y, axis=1, keepdims=True)
    nsend[...] = jnp.sum(jnp.where(diagonal, squares, 0.0), axis=0, keepdims=True)
    np_recv[plane] = nsend[...]
    for k in range(1, 32):
        send(nsend, np_recv.at[plane], NORM_P, plane_peer(k))
    arrived(np_recv.at[pl.ds(0, 31)], NORM_P)
    nz_send[...] = jnp.sum(np_recv[...], axis=0)
    nz_recv[z] = nz_send[...]
    for k in range(1, 16):
        send(nz_send, nz_recv.at[z], NORM_Z, z_peer(k))
    arrived(nz_recv.at[pl.ds(0, 15)], NORM_Z)
    total = jnp.sum(nz_recv[...], axis=0)
    mean = jnp.sum(jnp.where(diagonal, total, 0.0), axis=1, keepdims=True) / POINTS
    out_ref[...] = y / jnp.sqrt(mean + 1e-06)

    sent(xh, PTS)
    sent(s_recv.at[pl.ds(0, 7)], SRC)
    sent(t_recv.at[pl.ds(0, 7)], TGT)
    for i in range(3):
        sent(precv.at[i, pl.ds(0, 31)], PLANE + i)
        sent(zrecv.at[i, pl.ds(0, 15)], ZED + i)
        sent(xrecv.at[i, pl.ds(0, 3)], EX + i)
        sent(crecv.at[i, pl.ds(0, 7)], CO + i)
        sent(grecv.at[i, pl.ds(0, 7)], FAR + i)
        sent(vh.at[i], HALO + i)
    sent(np_recv.at[pl.ds(0, 31)], NORM_P)
    sent(nz_recv.at[pl.ds(0, 15)], NORM_Z)


def on_device(vectors, points, near_lists, inter_lists, skeleton, interp, transfer, coarse_points):
    vmem = pl.BlockSpec(memory_space=pltpu.VMEM)
    smem = pl.BlockSpec(memory_space=pltpu.SMEM)
    V = pltpu.VMEM
    return pl.pallas_call(
        kernel,
        out_shape=jax.ShapeDtypeStruct((16, 1024), F32),
        in_specs=[vmem, vmem, smem, smem, vmem, vmem, vmem, vmem],
        out_specs=vmem,
        scratch_shapes=[
            V((8, 1024), F32),
            V((2, 8, 1024), F32),
            V((3, 2, 16, 1024), F32),
            V((2, 16, 1024), F32),
            V((32, 3072), BF16),
            V((16, 1024), F32),
            V((256, 1024), BF16),
            V((256, 1024), BF16),
            V((1024, 256), BF16),
            V((1024, 256), BF16),
            V((128, 1024), BF16),
            V((1024, 128), BF16),
            V((3072, 1024), BF16),
            V((3072, 1024), BF16),
            V((8, 128), F32),
            V((8, 8, 128), F32),
            V((8, 24, 128), F32),
            V((8, 24, 128), F32),
            V((128, 1024), BF16),
            V((1024, 1024), BF16),
            V((1024, 1024), BF16),
            V((1024, 256), BF16),
            V((3, 4, 4, 128), F32),
            V((3, 32, 4, 128), F32),
            V((3, 4, 128), F32),
            V((3, 16, 4, 128), F32),
            V((3, 4, 128), F32),
            V((3, 4, 4, 128), F32),
            V((3, 16, 128), F32),
            V((3, 8, 16, 128), F32),
            V((3, 8, 16, 128), F32),
            V((3, 8, 16, 128), F32),
            V((1, 128), F32),
            V((32, 1, 128), F32),
            V((1, 128), F32),
            V((16, 1, 128), F32),
            pltpu.SemaphoreType.DMA((SEMS,)),
            pltpu.SemaphoreType.DMA((SEMS,)),
        ],
        compiler_params=pltpu.CompilerParams(
            collective_id=0, has_side_effects=True, vmem_limit_bytes=56 * 2**20
        ),
        name="filter",
    )(vectors, points, near_lists, inter_lists, skeleton, interp, transfer, coarse_points)


def solution(mesh):
    both = ("grp", "leaf")
    return jax.shard_map(
        on_device,
        mesh=mesh,
        in_specs=(
            P(None, both), P(None, both), P(both, None), P(both, None), P(both, None),
            P(both, None, None), P(both, None, None), P(),
        ),
        out_specs=P(None, both),
        check_vma=False,
    )
```

time: 381 us -> 91.4 us (0.24)
  the two profiles are of different devices: /device:TPU:32 before, /device:TPU:1 now
where the time goes in v1:
time: 91.4 us; the launch traced here: 91.2 us
  Pallas kernels  88.4 us (97%)
  local copies, waits for them, and re-layouts  2.79 us (3%)
    pallas_call x1, Pallas kernels, on_device(): pl.pallas_call(kernel, out_shape=jax.ShapeDtypeStruct((16, 1024), F32), i...  88.4 us
    unnamed x2, local copies, waits for them, and re-layouts  2.79 us

profile of v1, /device:TPU:1, one launch (start us, length us, event | category | flops | bytes accessed | tf_op | source)
XLA Modules:
  0.0 91.2 jit_solution(5938109353536890433)
XLA Ops:
  0.0 1.3 %copy.9.coarse_ref = f32[8,3,128]{2,1,0:T(4,128)} copy(f32[8,3,128]{2,0,1:T(8,128)} %param.15) | data formatting | bytes 24576 | tf_op args[7]
  1.3 88.4 %filter.1 = f32[16,1024]{1,0:T(8,128)} custom-call(f32[16,1024]{1,0:T(8,128)} %vec_ref.1, f32[3,1024]{1,0:T(4,128)} %pts_ref.1, s32[2,6]{1,0:T(2,128)} %near_ref.1, s32[2,16]{1,0:T(2,128)} %inter_ref.1, s32[2,64]{1,0:T(2,128)} %skel_ref.1, f32[2,64,512]{2,1,0:T(8,128)} %interp_ref.1, f32[2,64,128]{2,1,0:T(8,128)} %trans_ref.1, f32[8,3,128]{2,1,0:T(4,128)} %copy.9.coarse_ref), custom_call_target="tpu_custom_call" | custom-call | tf_op jit(solution)/shard_map/filter/pallas_call | solution.py:395
  89.7 1.5 %copy.11 = f32[16,1024]{1,0:T(8,128)} copy(f32[16,1024]{1,0:T(8,128)} %filter.1) | data formatting | bytes 131072

commit v2 on v1

--- a/solution.py
+++ b/solution.py
@@ -15,11 +15,19 @@
 POINTS = 524288
 SCALE = 3072.0
 PTS, SRC, TGT, HALO, CO, PLANE, ZED, EX, FAR, NORM_P, NORM_Z = 0, 1, 2, 3, 6, 9, 12, 15, 18, 21, 22
-SEMS = 23
+GRAM_Z, GRAM_X, GRAM_ALL, MIX = 23, 24, 25, 26
+SEMS = 27
+Z_ORDER = (8, 7, 9, 6, 10, 5, 11, 4, 12, 3, 13, 2, 14, 1, 15)
+C_ORDER = (4, 3, 5, 2, 6, 1, 7)
+PLANE_ORDER = (18, 17, 19, 16, 14, 22, 15, 13, 21, 23, 12, 20, 10, 26, 9, 11, 25, 27, 8, 24, 2, 30, 6, 1, 3, 5, 7, 29, 31, 28, 4)
 
 
 def dot(a, b):
     return jnp.dot(a, b, preferred_element_type=F32)
+
+
+def dot_t(a, b):
+    return lax.dot_general(a, b, (((1,), (1,)), ((), ())), preferred_element_type=F32)
 
 
 def split2(v):
@@ -73,11 +81,13 @@
 
 
 def kernel(
-    vec_ref, pts_ref, near_ref, inter_ref, skel_ref, interp_ref, trans_ref, coarse_ref, out_ref,
+    vec_in, pts_in, near_in, inter_in, skel_in, interp_in, trans_in, coarse_in, out_ref,
+    vec_ref, pts_ref, near_ref, inter_ref, skel_ref, interp_ref, trans_ref, coarse_ref,
     xs, xh, vh, ybuf, vcat, nacc, bhi, blo, bthi, btlo, tgt_near, src_f, khi, klo,
     s_send, s_recv, t_send, t_recv, tgt_far, fhi, flo, kc,
     usend, precv, wsend, zrecv, hsend, xrecv, csend, crecv, gsend, grecv,
-    nsend, np_recv, nz_send, nz_recv, send_sem, recv_sem,
+    nsend, np_recv, nz_send, nz_recv,
+    ga_send, ga_recv, gb_send, gb_recv, gc_send, gc_recv, gram, gram2, mx_send, mx_recv, send_sem, recv_sem, in_sem,
 ):
     g = lax.axis_index("grp")
     leaf = lax.axis_index("leaf")
@@ -119,6 +129,16 @@
 
     def sent(ref, sem):
         pltpu.make_async_copy(ref, ref, send_sem.at[sem]).wait()
+
+    loads = [
+        pltpu.make_async_copy(src, dst, in_sem.at[n])
+        for n, (src, dst) in enumerate((
+            (vec_in, vec_ref), (interp_in, interp_ref), (trans_in, trans_ref), (pts_in, pts_ref),
+            (skel_in, skel_ref), (near_in, near_ref), (inter_in, inter_ref), (coarse_in, coarse_ref),
+        ))
+    ]
+    for load in loads:
+        load.start()
 
     barrier = pltpu.get_barrier_semaphore()
 
@@ -134,60 +154,82 @@
     greet(right)
     greet(left)
 
+    for load in loads:
+        load.wait()
     xs[...] = jnp.zeros_like(xs)
     xs[0:3, :] = pts_ref[...]
     origin = xs[:, 0:1]
 
-    for l in range(2):
-        t_t = trans_ref[l].T
-        e = jnp.dot(t_t, interp_ref[l], precision=lax.Precision.HIGHEST, preferred_element_type=F32)
-        zero = jnp.zeros((64, 512), F32)
-        lower = [interp_ref[l], zero] if l == 0 else [zero, interp_ref[l]]
-        b = jnp.concatenate([e, *lower], axis=0)
-        hi, lo = split2(b)
-        bhi[:, l * 512 : (l + 1) * 512] = hi
-        blo[:, l * 512 : (l + 1) * 512] = lo
-        hi, lo = split2(b.T)
-        bthi[l * 512 : (l + 1) * 512, :] = hi
-        btlo[l * 512 : (l + 1) * 512, :] = lo
-
-    both = []
-    for l in range(2):
-        pick = lax.broadcasted_iota(jnp.int32, (512, 64), 0) == skel_ref[l : l + 1, :]
-        pick = jnp.where(pick, 1.0, 0.0).astype(BF16)
-        h, m, lo = split3(xs[:, l * 512 : (l + 1) * 512])
-        got = dot(jnp.concatenate([h, m, lo, jnp.zeros_like(h)], axis=0).astype(BF16), pick)
-        both.append(got[0:8] + (got[8:16] + got[16:24]))
-    skel = jnp.concatenate(both, axis=1)
-    s_send[...] = skel
-    s_recv[rho] = skel
-
-    row = lax.broadcasted_iota(jnp.int32, (128, 128), 0)
-    number = ((row >> 2) & 3) * 32 + (row >> 4) * 4 + (row & 3)
-    first = lax.broadcasted_iota(jnp.int32, (1, 128), 1) < 64
-    listed = jnp.zeros((128, 128), F32)
-    for s in range(16):
-        wanted = jnp.where(first, inter_ref[0, s], inter_ref[1, s])
-        listed = jnp.where(number == wanted, 1.0, listed)
-    off = (1.0 - listed) * FAR_AWAY
-    for j in range(8):
-        t_send[j, 0:8, :] = skel
-        t_send[j, 8:24, :] = off[j * 16 : (j + 1) * 16]
-    t_recv[zh] = t_send[zh]
+    def bases():
+        for l in range(2):
+            t_t = trans_ref[l].T
+            e = jnp.dot(t_t, interp_ref[l], precision=lax.Precision.HIGHEST, preferred_element_type=F32)
+            zero = jnp.zeros((64, 512), F32)
+            lower = [interp_ref[l], zero] if l == 0 else [zero, interp_ref[l]]
+            b = jnp.concatenate([e, *lower], axis=0)
+            hi, lo = split2(b)
+            bhi[:, l * 512 : (l + 1) * 512] = hi
+            blo[:, l * 512 : (l + 1) * 512] = lo
+            hi, lo = split2(b.T)
+            bthi[l * 512 : (l + 1) * 512, :] = hi
+            btlo[l * 512 : (l + 1) * 512, :] = lo
+
+    def skeletons():
+        both = []
+        for l in range(2):
+            pick = lax.broadcasted_iota(jnp.int32, (512, 64), 0) == skel_ref[l : l + 1, :]
+            pick = jnp.where(pick, 1.0, 0.0).astype(BF16)
+            h, m, lo = split3(xs[:, l * 512 : (l + 1) * 512])
+            got = dot(jnp.concatenate([h, m, lo, jnp.zeros_like(h)], axis=0).astype(BF16), pick)
+            both.append(got[0:8] + (got[8:16] + got[16:24]))
+        skel = jnp.concatenate(both, axis=1)
+        s_send[...] = skel
+        s_recv[rho] = skel
+
+        row = lax.broadcasted_iota(jnp.int32, (128, 128), 0)
+        number = ((row >> 2) & 3) * 32 + (row >> 4) * 4 + (row & 3)
+        first = lax.broadcasted_iota(jnp.int32, (1, 128), 1) < 64
+        listed = jnp.zeros((128, 128), F32)
+        for s in range(16):
+            wanted = jnp.where(first, inter_ref[0, s], inter_ref[1, s])
+            listed = jnp.where(number == wanted, 1.0, listed)
+        off = (1.0 - listed) * FAR_AWAY
+        for j in range(8):
+            t_send[j, 0:8, :] = skel
+            t_send[j, 8:24, :] = off[j * 16 : (j + 1) * 16]
+        t_recv[zh] = t_send[zh]
 
     def split_field(y):
         vcat[:, 1024:2048] = stacked(y)
 
+    def keep_plane(i, u):
+        for j in range(4):
+            usend[i, j] = u[4 * j : 4 * j + 4]
+        precv[i, plane] = usend[i, x]
+
+    def keep_coeffs(i, c):
+        csend[i] = c
+        crecv[i, rho] = c
+
+    def keep_upward(i, u, c):
+        keep_plane(i, u)
+        keep_coeffs(i, c)
+
     def upward(i):
         uc = dot3(vcat[:, 1024:2048], bthi[...], btlo[...])
-        for j in range(4):
-            usend[i, j] = uc[4 * j : 4 * j + 4, 0:128]
-        precv[i, plane] = usend[i, x]
-        csend[i] = uc[:, 128:256]
-        crecv[i, rho] = uc[:, 128:256]
+        keep_upward(i, uc[:, 0:128], uc[:, 128:256])
+
+    def exact(a, b, contract):
+        return lax.dot_general(
+            a, b, (((1,), (contract,)), ((), ())), precision=lax.Precision.HIGHEST, preferred_element_type=F32
+        )
+
+    def first_upward():
+        c = [exact(vec_ref[:, l * 512 : (l + 1) * 512], interp_ref[l], 1) for l in range(2)]
+        keep_upward(0, exact(c[0], trans_ref[0], 0) + exact(c[1], trans_ref[1], 0), jnp.concatenate(c, axis=1))
 
     def send_plane(i):
-        for k in range(1, 32):
+        for k in PLANE_ORDER:
             send(usend.at[i, lax.rem(plane_index(k), 4)], precv.at[i, plane], PLANE + i, plane_peer(k))
 
     def send_coeffs(i):
@@ -197,29 +239,72 @@
     def send_halo(i, field):
         send(field, vh.at[i, 0], HALO + i, right)
         send(field, vh.at[i, 1], HALO + i, left)
+
+    def couple(c4, w2):
+        hi = c4.astype(BF16).astype(F32)
+        lhs = jnp.concatenate([hi, c4 - hi, jnp.zeros((8, c4.shape[1]), F32)], axis=0).astype(BF16)
+        r = dot(lhs, w2[...])
+        return r[0:4, 0:128] + r[4:8, 0:128] + r[0:4, 128:256]
 
     def plane_to_z(i):
         arrived(precv.at[i, pl.ds(0, 31)], PLANE + i)
         cols = []
         for e in range(8):
             cols.append((precv[i, 4 * e] + precv[i, 4 * e + 1]) + (precv[i, 4 * e + 2] + precv[i, 4 * e + 3]))
-        c4 = jnp.concatenate(cols, axis=1)
-        hi = c4.astype(BF16).astype(F32)
-        lhs = jnp.concatenate([hi, c4 - hi, jnp.zeros((8, 1024), F32)], axis=0).astype(BF16)
-        r = dot(lhs, kc[...])
-        w = r[0:4, 0:128] + r[4:8, 0:128] + r[0:4, 128:256]
+        w = couple(jnp.concatenate(cols, axis=1), kc)
         wsend[i] = w
         zrecv[i, z] = w
-        for k in range(1, 16):
+        for k in Z_ORDER:
             send(wsend.at[i], zrecv.at[i, z], ZED + i, z_peer(k))
 
-    def z_to_x(i):
+    def z_to_x(i, more=0.0):
         arrived(zrecv.at[i, pl.ds(0, 15)], ZED + i)
-        h = jnp.sum(zrecv[i], axis=0)
+        h = jnp.sum(zrecv[i], axis=0) + more
         hsend[i] = h
         xrecv[i, x] = h
         for k in range(1, 4):
             send(hsend.at[i], xrecv.at[i, x], EX + i, x_peer(k))
+
+    def gram_own():
+        e, f = bhi[0:128, :], blo[0:128, :]
+        m = dot_t(e, e) + (dot_t(e, f) + dot_t(f, e))
+        for j in range(16):
+            ga_send[j] = m[j * 8 : (j + 1) * 8]
+        ga_recv[z] = ga_send[z]
+        for k in Z_ORDER:
+            send(ga_send.at[lax.rem(z + k, 16)], ga_recv.at[z], GRAM_Z, z_peer(k))
+
+    def gram_x():
+        arrived(ga_recv.at[pl.ds(0, 15)], GRAM_Z)
+        m = jnp.sum(ga_recv[...], axis=0)
+        gb_send[...] = m
+        gb_recv[x] = m
+        for k in range(1, 4):
+            send(gb_send, gb_recv.at[x], GRAM_X, x_peer(k))
+
+    def gram_all():
+        arrived(gb_recv.at[pl.ds(0, 3)], GRAM_X)
+        m = jnp.sum(gb_recv[...], axis=0)
+        gc_send[...] = m
+        gc_recv[z] = m
+        for k in Z_ORDER:
+            send(gc_send, gc_recv.at[z], GRAM_ALL, z_peer(k))
+
+    def mix_send():
+        arrived(gc_recv.at[pl.ds(0, 15)], GRAM_ALL)
+        for j in range(16):
+            gram[j * 8 : (j + 1) * 8, :] = gc_recv[j]
+        hi, lo = split2(gram[...])
+        gram2[:, 0:128] = hi
+        gram2[:, 128:256] = lo
+        mx_send[...] = couple(hsend[1], gram2)
+        mx_recv[g] = mx_send[...]
+        for k in (4, 3, 5, 2, 6, 1, 7):
+            send(mx_send, mx_recv.at[g], MIX, (lax.rem(g + k, 8), leaf))
+
+    def mix():
+        arrived(mx_recv.at[pl.ds(0, 7)], MIX)
+        return couple(jnp.concatenate([mx_recv[e] for e in range(8)], axis=1), kc)
 
     def far_partial(i):
         arrived(crecv.at[i, pl.ds(0, 7)], CO + i)
@@ -228,7 +313,7 @@
         for j in range(8):
             gsend[i, j] = part[:, j * 128 : (j + 1) * 128]
         grecv[i, zh] = gsend[i, zh]
-        for k in range(1, 8):
+        for k in C_ORDER:
             send(gsend.at[i, lax.rem(zh + k, 8)], grecv.at[i, zh], FAR + i, c_peer(k))
 
     def near(lo, hi):
@@ -239,11 +324,17 @@
         vcat[:, 0:1024] = stacked(vh[i, 0])
         vcat[:, 2048:3072] = stacked(vh[i, 1])
 
+    def leaf_far(i):
+        arrived(grecv.at[i, pl.ds(0, 7)], FAR + i)
+        return jnp.sum(grecv[i], axis=0)
+
+    def coarse_field(i):
+        arrived(xrecv.at[i, pl.ds(0, 3)], EX + i)
+        return jnp.concatenate([xrecv[i, j] for j in range(4)], axis=0)
+
     def downward(i):
-        arrived(grecv.at[i, pl.ds(0, 7)], FAR + i)
-        gq = jnp.sum(grecv[i], axis=0)
-        arrived(xrecv.at[i, pl.ds(0, 3)], EX + i)
-        h = jnp.concatenate([xrecv[i, j] for j in range(4)], axis=0)
+        gq = leaf_far(i)
+        h = coarse_field(i)
         return (nacc[...] + dot3(stacked(jnp.concatenate([h, gq], axis=1)), bhi[...], blo[...])) / SCALE
 
     def local(v):
@@ -289,23 +380,23 @@
     def coarse_kernel():
         none = jnp.zeros((8, 128), F32)
         pad = jnp.zeros((5, 128), F32)
-        own = (jnp.concatenate([coarse_ref[g], pad], axis=0) - 0.5) * ALPHA
+        own = (jnp.concatenate([coarse_ref[d, pl.ds(g, 1), :] for d in range(3)] + [pad], axis=0) - 0.5) * ALPHA
         tgt = target_features(own, none)
         for e in range(8):
-            q = (jnp.concatenate([coarse_ref[e], pad], axis=0) - 0.5) * ALPHA
+            q = (jnp.concatenate([coarse_ref[d, e : e + 1, :] for d in range(3)] + [pad], axis=0) - 0.5) * ALPHA
             k = matern(dot(source_features(q, none).T.astype(BF16), tgt))
             k = k * jnp.where(g == e, 0.0, 1.0)
             hi, lo = split2(k)
             kc[e * 128 : (e + 1) * 128, 0:128] = hi
             kc[e * 128 : (e + 1) * 128, 128:256] = lo
 
-    split_field(vec_ref[...])
-    upward(0)
+    first_upward()
 
     pl.semaphore_wait(barrier, 15 + 31 + 7 + 2)
 
     send_plane(0)
-    for k in range(1, 8):
+    skeletons()
+    for k in C_ORDER:
         send(t_send.at[lax.rem(zh + k, 8)], t_recv.at[zh], TGT, c_peer(k))
     for k in range(1, 8):
         send(s_send, s_recv.at[rho], SRC, r_peer(k))
@@ -314,6 +405,7 @@
     send(xs, xh.at[1], PTS, left)
     send_halo(0, vec_ref)
 
+    split_field(vec_ref[...])
     coarse_kernel()
     r = lax.broadcasted_iota(jnp.int32, (8, 1024), 0)
     first = lax.broadcasted_iota(jnp.int32, (1, 1024), 1) < 512
@@ -324,11 +416,12 @@
     near_features(xs[...], 2)
     near_kernel(1024)
     plane_to_z(0)
-    nacc[...] = near(1024, 2048)
     arrived(s_recv.at[pl.ds(0, 7)], SRC)
     arrived(t_recv.at[pl.ds(0, 7)], TGT)
     far_kernel()
     far_partial(0)
+    bases()
+    nacc[...] = near(1024, 2048)
     arrived(xh, PTS)
     near_features(xh[0], 0)
     near_kernel(0)
@@ -340,41 +433,52 @@
     y = (downward(0) - CENTRE * vec_ref[...]) / HALF_WIDTH
     ybuf[0] = y
 
-    for i in (1, 2):
-        split_field(ybuf[i - 1])
-        upward(i)
-        send_plane(i)
-        send_coeffs(i)
-        send_halo(i, ybuf.at[i - 1])
-        nacc[...] = near(1024, 2048)
-        far_partial(i)
-        plane_to_z(i)
-        take_halo(i)
-        nacc[...] += near(0, 1024) + near(2048, 3072)
-        z_to_x(i)
-        before = vec_ref[...] if i == 1 else ybuf[0]
-        y = 2.0 * (downward(i) - CENTRE * ybuf[i - 1]) / HALF_WIDTH - before
-        if i == 1:
-            ybuf[1] = y
+    gain = 2.0 / (HALF_WIDTH * SCALE)
+    split_field(ybuf[0])
+    upward(1)
+    send_plane(1)
+    send_coeffs(1)
+    send_halo(1, ybuf.at[0])
+    nacc[...] = near(1024, 2048)
+    gram_own()
+    far_partial(1)
+    plane_to_z(1)
+    take_halo(1)
+    nacc[...] += near(0, 1024) + near(2048, 3072)
+    gram_x()
+    z_to_x(1)
+    part = nacc[...] + dot3(stacked(leaf_far(1)), bhi[128:256, :], blo[128:256, :])
+    part = gain * part - (2.0 * CENTRE / HALF_WIDTH) * ybuf[0] - vec_ref[...]
+    keep_plane(2, dot3(stacked(part), bthi[:, 0:128], btlo[:, 0:128]))
+    send_plane(2)
+    gram_all()
+    y = part + gain * dot3(stacked(coarse_field(1)), bhi[0:128, :], blo[0:128, :])
+    ybuf[1] = y
+    split_field(y)
+    keep_coeffs(2, dot3(vcat[:, 1024:2048], bthi[:, 128:256], btlo[:, 128:256]))
+    send_coeffs(2)
+    send_halo(2, ybuf.at[1])
+    nacc[...] = near(1024, 2048)
+    plane_to_z(2)
+    far_partial(2)
+    mix_send()
+    take_halo(2)
+    nacc[...] += near(0, 1024) + near(2048, 3072)
+    z_to_x(2, gain * mix())
+    y = 2.0 * (downward(2) - CENTRE * ybuf[1]) / HALF_WIDTH - ybuf[0]
 
     lane = lax.broadcasted_iota(jnp.int32, (16, 128), 1)
     diagonal = lane == lax.broadcasted_iota(jnp.int32, (16, 128), 0)
     squares = jnp.sum(y * y, axis=1, keepdims=True)
     nsend[...] = jnp.sum(jnp.where(diagonal, squares, 0.0), axis=0, keepdims=True)
     np_recv[plane] = nsend[...]
-    for k in range(1, 32):
+    for k in PLANE_ORDER:
         send(nsend, np_recv.at[plane], NORM_P, plane_peer(k))
-    arrived(np_recv.at[pl.ds(0, 31)], NORM_P)
-    nz_send[...] = jnp.sum(np_recv[...], axis=0)
-    nz_recv[z] = nz_send[...]
-    for k in range(1, 16):
-        send(nz_send, nz_recv.at[z], NORM_Z, z_peer(k))
-    arrived(nz_recv.at[pl.ds(0, 15)], NORM_Z)
-    total = jnp.sum(nz_recv[...], axis=0)
-    mean = jnp.sum(jnp.where(diagonal, total, 0.0), axis=1, keepdims=True) / POINTS
-    out_ref[...] = y / jnp.sqrt(mean + 1e-06)
-
     sent(xh, PTS)
+    sent(ga_recv.at[pl.ds(0, 15)], GRAM_Z)
+    sent(gb_recv.at[pl.ds(0, 3)], GRAM_X)
+    sent(gc_recv.at[pl.ds(0, 15)], GRAM_ALL)
+    sent(mx_recv.at[pl.ds(0, 7)], MIX)
     sent(s_recv.at[pl.ds(0, 7)], SRC)
     sent(t_recv.at[pl.ds(0, 7)], TGT)
     for i in range(3):
@@ -384,20 +488,37 @@
         sent(crecv.at[i, pl.ds(0, 7)], CO + i)
         sent(grecv.at[i, pl.ds(0, 7)], FAR + i)
         sent(vh.at[i], HALO + i)
+    arrived(np_recv.at[pl.ds(0, 31)], NORM_P)
+    nz_send[...] = jnp.sum(np_recv[...], axis=0)
+    nz_recv[z] = nz_send[...]
+    for k in Z_ORDER:
+        send(nz_send, nz_recv.at[z], NORM_Z, z_peer(k))
+    arrived(nz_recv.at[pl.ds(0, 15)], NORM_Z)
+    total = jnp.sum(nz_recv[...], axis=0)
+    mean = jnp.sum(jnp.where(diagonal, total, 0.0), axis=1, keepdims=True) / POINTS
+    out_ref[...] = y / jnp.sqrt(mean + 1e-06)
+
     sent(np_recv.at[pl.ds(0, 31)], NORM_P)
     sent(nz_recv.at[pl.ds(0, 15)], NORM_Z)
 
 
 def on_device(vectors, points, near_lists, inter_lists, skeleton, interp, transfer, coarse_points):
     vmem = pl.BlockSpec(memory_space=pltpu.VMEM)
-    smem = pl.BlockSpec(memory_space=pltpu.SMEM)
     V = pltpu.VMEM
     return pl.pallas_call(
         kernel,
         out_shape=jax.ShapeDtypeStruct((16, 1024), F32),
-        in_specs=[vmem, vmem, smem, smem, vmem, vmem, vmem, vmem],
+        in_specs=[pl.BlockSpec(memory_space=pl.ANY)] * 8,
         out_specs=vmem,
         scratch_shapes=[
+            V((16, 1024), F32),
+            V((3, 1024), F32),
+            pltpu.SMEM((2, 6), jnp.int32),
+            pltpu.SMEM((2, 16), jnp.int32),
+            V((2, 64), jnp.int32),
+            V((2, 64, 512), F32),
+            V((2, 64, 128), F32),
+            V((3, 8, 128), F32),
             V((8, 1024), F32),
             V((2, 8, 1024), F32),
             V((3, 2, 16, 1024), F32),
@@ -434,14 +555,25 @@
             V((32, 1, 128), F32),
             V((1, 128), F32),
             V((16, 1, 128), F32),
+            V((16, 8, 128), F32),
+            V((16, 8, 128), F32),
+            V((8, 128), F32),
+            V((4, 8, 128), F32),
+            V((8, 128), F32),
+            V((16, 8, 128), F32),
+            V((128, 128), F32),
+            V((128, 256), BF16),
+            V((4, 128), F32),
+            V((8, 4, 128), F32),
             pltpu.SemaphoreType.DMA((SEMS,)),
             pltpu.SemaphoreType.DMA((SEMS,)),
+            pltpu.SemaphoreType.DMA((8,)),
         ],
         compiler_params=pltpu.CompilerParams(
             collective_id=0, has_side_effects=True, vmem_limit_bytes=56 * 2**20
         ),
         name="filter",
-    )(vectors, points, near_lists, inter_lists, skeleton, interp, transfer, coarse_points)
+    )(vectors, points, near_lists, inter_lists, skeleton, interp, transfer, coarse_points.transpose(1, 0, 2))
 
 
 def solution(mesh):

time: 91.4 us -> 84.8 us (0.928)
  Pallas kernels: 88.4 us -> 83.2 us
  local copies, waits for them, and re-layouts: 2.79 us -> 1.47 us
    pallas_call x1, Pallas kernels: 88.4 us -> 83.2 us  [on_device(): pl.pallas_call(kernel, out_shape=jax.ShapeDtypeStruct((16, 1024), F32), i...]
    unnamed x2 -> x1, local copies, waits for them, and re-layouts: 2.79 us -> 1.47 us
where the time goes in v2:
time: 84.8 us; the launch traced here: 84.7 us
  Pallas kernels  83.2 us (98%)
  local copies, waits for them, and re-layouts  1.47 us (2%)
    pallas_call x1, Pallas kernels, on_device(): pl.pallas_call(kernel, out_shape=jax.ShapeDtypeStruct((16, 1024), F32), i...  83.2 us

profile of v2, /device:TPU:1, one launch (start us, length us, event | category | flops | bytes accessed | tf_op | source)
XLA Modules:
  0.0 84.7 jit_solution(1946195522687757595)
XLA Ops:
  0.0 83.2 %filter.1 = f32[16,1024]{1,0:T(8,128)} custom-call(f32[16,1024]{1,0:T(8,128)} %vec_in.1, f32[3,1024]{1,0:T(4,128)} %pts_in.1, s32[2,6]{1,0:T(2,128)} %near_in.1, s32[2,16]{1,0:T(2,128)} %inter_in.1, s32[2,64]{1,0:T(2,128)} %skel_in.1, f32[2,64,512]{2,1,0:T(8,128)} %interp_in.1, f32[2,64,128]{2,1,0:T(8,128)} %trans_in.1, f32[3,8,128]{2,1,0:T(8,128)} %bitcast.1), custom_call_target="tpu_custom_call" | custom-call | tf_op jit(solution)/shard_map/filter/pallas_call | solution.py:508
  83.2 1.5 %copy.10 = f32[16,1024]{1,0:T(8,128)} copy(f32[16,1024]{1,0:T(8,128)} %filter.1) | data formatting | bytes 131072

commit v3 on v2

--- a/solution.py
+++ b/solution.py
@@ -83,7 +83,7 @@
 def kernel(
     vec_in, pts_in, near_in, inter_in, skel_in, interp_in, trans_in, coarse_in, out_ref,
     vec_ref, pts_ref, near_ref, inter_ref, skel_ref, interp_ref, trans_ref, coarse_ref,
-    xs, xh, vh, ybuf, vcat, nacc, bhi, blo, bthi, btlo, tgt_near, src_f, khi, klo,
+    xs, xh, vh, ybuf, vcat, nacc, bhi, blo, bthi, btlo, tgt_near, src_f, far_f, khi, klo,
     s_send, s_recv, t_send, t_recv, tgt_far, fhi, flo, kc,
     usend, precv, wsend, zrecv, hsend, xrecv, csend, crecv, gsend, grecv,
     nsend, np_recv, nz_send, nz_recv,
@@ -346,36 +346,39 @@
         f = source_features(local(points), jnp.where(r == place, 1.0, 0.0))
         src_f[...] = f.T.astype(BF16)
 
-    def near_kernel(base):
+    def near_kernel(base, first=0, last=2):
         def body(i, _):
-            r = pl.multiple_of(i * 256, 256)
+            r = pl.multiple_of(i * 512, 512)
             for c in (0, 512):
-                k = matern(dot(src_f[pl.ds(r, 256), :], tgt_near[:, c : c + 512]))
+                k = matern(dot(src_f[pl.ds(r, 512), :], tgt_near[:, c : c + 512]))
                 hi, lo = split2(k)
-                khi[pl.ds(base + r, 256), c : c + 512] = hi
-                klo[pl.ds(base + r, 256), c : c + 512] = lo
+                khi[pl.ds(base + r, 512), c : c + 512] = hi
+                klo[pl.ds(base + r, 512), c : c + 512] = lo
             return 0
 
-        lax.fori_loop(0, 4, body, 0)
-
-    def far_kernel():
+        lax.fori_loop(first, last, body, 0)
+
+    def far_sources():
         half = lax.broadcasted_iota(jnp.int32, (16, 128), 1) // 64
         r = lax.broadcasted_iota(jnp.int32, (16, 128), 0)
         for j in range(8):
             f = source_features(local(s_recv[j]), jnp.where(r == 2 * j + half, 1.0, 0.0))
-            src_f[j * 128 : (j + 1) * 128, :] = f.T.astype(BF16)
+            far_f[j * 128 : (j + 1) * 128, :] = f.T.astype(BF16)
+
+    def far_kernel():
+        for j in range(8):
             tgt_far[:, j * 128 : (j + 1) * 128] = target_features(local(t_recv[j, 0:8, :]), t_recv[j, 8:24, :])
 
         def body(i, _):
-            r = pl.multiple_of(i * 256, 256)
+            r = pl.multiple_of(i * 512, 512)
             for c in (0, 512):
-                k = matern(dot(src_f[pl.ds(r, 256), :], tgt_far[:, c : c + 512]))
+                k = matern(dot(far_f[pl.ds(r, 512), :], tgt_far[:, c : c + 512]))
                 hi, lo = split2(k)
-                fhi[pl.ds(r, 256), c : c + 512] = hi
-                flo[pl.ds(r, 256), c : c + 512] = lo
+                fhi[pl.ds(r, 512), c : c + 512] = hi
+                flo[pl.ds(r, 512), c : c + 512] = lo
             return 0
 
-        lax.fori_loop(0, 4, body, 0)
+        lax.fori_loop(0, 2, body, 0)
 
     def coarse_kernel():
         none = jnp.zeros((8, 128), F32)
@@ -391,20 +394,7 @@
             kc[e * 128 : (e + 1) * 128, 128:256] = lo
 
     first_upward()
-
-    pl.semaphore_wait(barrier, 15 + 31 + 7 + 2)
-
-    send_plane(0)
     skeletons()
-    for k in C_ORDER:
-        send(t_send.at[lax.rem(zh + k, 8)], t_recv.at[zh], TGT, c_peer(k))
-    for k in range(1, 8):
-        send(s_send, s_recv.at[rho], SRC, r_peer(k))
-    send_coeffs(0)
-    send(xs, xh.at[0], PTS, right)
-    send(xs, xh.at[1], PTS, left)
-    send_halo(0, vec_ref)
-
     split_field(vec_ref[...])
     coarse_kernel()
     r = lax.broadcasted_iota(jnp.int32, (8, 1024), 0)
@@ -414,14 +404,29 @@
         listed = jnp.where(r == jnp.where(first, near_ref[0, s], near_ref[1, s]), 1.0, listed)
     tgt_near[...] = target_features(local(xs[...]), (1.0 - listed) * FAR_AWAY)
     near_features(xs[...], 2)
-    near_kernel(1024)
+    bases()
+    near_kernel(1024, 0, 1)
+
+    pl.semaphore_wait(barrier, 15 + 31 + 7 + 2)
+
+    for k in C_ORDER:
+        send(t_send.at[lax.rem(zh + k, 8)], t_recv.at[zh], TGT, c_peer(k))
+    send_plane(0)
+    for k in range(1, 8):
+        send(s_send, s_recv.at[rho], SRC, r_peer(k))
+    send_coeffs(0)
+    send(xs, xh.at[0], PTS, right)
+    send(xs, xh.at[1], PTS, left)
+    send_halo(0, vec_ref)
+
+    near_kernel(1024, 1, 2)
+    arrived(s_recv.at[pl.ds(0, 7)], SRC)
+    far_sources()
     plane_to_z(0)
-    arrived(s_recv.at[pl.ds(0, 7)], SRC)
+    nacc[...] = near(1024, 2048)
     arrived(t_recv.at[pl.ds(0, 7)], TGT)
     far_kernel()
     far_partial(0)
-    bases()
-    nacc[...] = near(1024, 2048)
     arrived(xh, PTS)
     near_features(xh[0], 0)
     near_kernel(0)
@@ -447,11 +452,11 @@
     nacc[...] += near(0, 1024) + near(2048, 3072)
     gram_x()
     z_to_x(1)
+    gram_all()
     part = nacc[...] + dot3(stacked(leaf_far(1)), bhi[128:256, :], blo[128:256, :])
     part = gain * part - (2.0 * CENTRE / HALF_WIDTH) * ybuf[0] - vec_ref[...]
     keep_plane(2, dot3(stacked(part), bthi[:, 0:128], btlo[:, 0:128]))
     send_plane(2)
-    gram_all()
     y = part + gain * dot3(stacked(coarse_field(1)), bhi[0:128, :], blo[0:128, :])
     ybuf[1] = y
     split_field(y)
@@ -459,9 +464,9 @@
     send_coeffs(2)
     send_halo(2, ybuf.at[1])
     nacc[...] = near(1024, 2048)
+    mix_send()
     plane_to_z(2)
     far_partial(2)
-    mix_send()
     take_halo(2)
     nacc[...] += near(0, 1024) + near(2048, 3072)
     z_to_x(2, gain * mix())
@@ -530,6 +535,7 @@
             V((1024, 256), BF16),
             V((1024, 256), BF16),
             V((128, 1024), BF16),
+            V((1024, 128), BF16),
             V((1024, 128), BF16),
             V((3072, 1024), BF16),
             V((3072, 1024), BF16),

time: 84.8 us -> 82.1 us (0.968)
  Pallas kernels: 83.2 us -> 80.4 us
    pallas_call x1, Pallas kernels: 83.2 us -> 80.4 us  [on_device(): pl.pallas_call(kernel, out_shape=jax.ShapeDtypeStruct((16, 1024), F32), i...]
where the time goes in v3:
time: 82.1 us; the launch traced here: 81.9 us
  Pallas kernels  80.4 us (98%)
  local copies, waits for them, and re-layouts  1.47 us (2%)
    pallas_call x1, Pallas kernels, on_device(): pl.pallas_call(kernel, out_shape=jax.ShapeDtypeStruct((16, 1024), F32), i...  80.4 us

profile of v3, /device:TPU:1, one launch (start us, length us, event | category | flops | bytes accessed | tf_op | source)
XLA Modules:
  0.0 81.9 jit_solution(6463403783207077094)
XLA Ops:
  0.0 80.4 %filter.1 = f32[16,1024]{1,0:T(8,128)} custom-call(f32[16,1024]{1,0:T(8,128)} %vec_in.1, f32[3,1024]{1,0:T(4,128)} %pts_in.1, s32[2,6]{1,0:T(2,128)} %near_in.1, s32[2,16]{1,0:T(2,128)} %inter_in.1, s32[2,64]{1,0:T(2,128)} %skel_in.1, f32[2,64,512]{2,1,0:T(8,128)} %interp_in.1, f32[2,64,128]{2,1,0:T(8,128)} %trans_in.1, f32[3,8,128]{2,1,0:T(8,128)} %bitcast.1), custom_call_target="tpu_custom_call" | custom-call | tf_op jit(solution)/shard_map/filter/pallas_call | solution.py:513
  80.4 1.5 %copy.10 = f32[16,1024]{1,0:T(8,128)} copy(f32[16,1024]{1,0:T(8,128)} %filter.1) | data formatting | bytes 131072

commit v4 on v3

--- a/solution.py
+++ b/solution.py
@@ -19,7 +19,7 @@
 SEMS = 27
 Z_ORDER = (8, 7, 9, 6, 10, 5, 11, 4, 12, 3, 13, 2, 14, 1, 15)
 C_ORDER = (4, 3, 5, 2, 6, 1, 7)
-PLANE_ORDER = (18, 17, 19, 16, 14, 22, 15, 13, 21, 23, 12, 20, 10, 26, 9, 11, 25, 27, 8, 24, 2, 30, 6, 1, 3, 5, 7, 29, 31, 28, 4)
+PLANE_ORDER = (14, 18, 22, 6, 10, 13, 15, 17, 19, 21, 23, 26, 30, 2, 5, 7, 9, 11, 12, 16, 20, 25, 27, 29, 31, 1, 3, 4, 8, 24, 28)
 
 
 def dot(a, b):
@@ -96,18 +96,20 @@
     plane = g * 4 + x
     rho = x * 2 + zl
 
+    groups = [lax.rem(g + k, 8) for k in range(8)]
+    columns = [lax.rem(x + k, 4) for k in range(4)]
+    leaves = [c * 16 + z for c in columns]
+    levels = [lax.rem(z + k, 16) for k in range(16)]
+    z_leaves = [x * 16 + n for n in levels]
+
     def z_peer(k):
-        return (g, x * 16 + lax.rem(z + k, 16))
-
-    def plane_index(k):
-        return lax.rem(plane + k, 32)
+        return (g, z_leaves[k])
 
     def plane_peer(k):
-        i = plane_index(k)
-        return (i // 4, lax.rem(i, 4) * 16 + z)
+        return (groups[k // 4], leaves[k % 4])
 
     def x_peer(k):
-        return (g, lax.rem(x + k, 4) * 16 + z)
+        return (g, leaves[k])
 
     def r_peer(k):
         i = lax.rem(rho + k, 8)
@@ -145,9 +147,9 @@
     def greet(peer):
         pl.semaphore_signal(barrier, inc=1, device_id=peer, device_id_type=MESH)
 
-    for k in range(1, 16):
+    for k in Z_ORDER:
         greet(z_peer(k))
-    for k in range(1, 32):
+    for k in PLANE_ORDER:
         greet(plane_peer(k))
     for k in range(1, 8):
         greet(r_peer(k))
@@ -230,7 +232,7 @@
 
     def send_plane(i):
         for k in PLANE_ORDER:
-            send(usend.at[i, lax.rem(plane_index(k), 4)], precv.at[i, plane], PLANE + i, plane_peer(k))
+            send(usend.at[i, columns[k % 4]], precv.at[i, plane], PLANE + i, plane_peer(k))
 
     def send_coeffs(i):
         for k in range(1, 8):
@@ -272,7 +274,7 @@
             ga_send[j] = m[j * 8 : (j + 1) * 8]
         ga_recv[z] = ga_send[z]
         for k in Z_ORDER:
-            send(ga_send.at[lax.rem(z + k, 16)], ga_recv.at[z], GRAM_Z, z_peer(k))
+            send(ga_send.at[levels[k]], ga_recv.at[z], GRAM_Z, z_peer(k))
 
     def gram_x():
         arrived(ga_recv.at[pl.ds(0, 15)], GRAM_Z)
@@ -300,7 +302,7 @@
         mx_send[...] = couple(hsend[1], gram2)
         mx_recv[g] = mx_send[...]
         for k in (4, 3, 5, 2, 6, 1, 7):
-            send(mx_send, mx_recv.at[g], MIX, (lax.rem(g + k, 8), leaf))
+            send(mx_send, mx_recv.at[g], MIX, (groups[k], leaf))
 
     def mix():
         arrived(mx_recv.at[pl.ds(0, 7)], MIX)
@@ -441,12 +443,12 @@
     gain = 2.0 / (HALF_WIDTH * SCALE)
     split_field(ybuf[0])
     upward(1)
+    send_coeffs(1)
     send_plane(1)
-    send_coeffs(1)
     send_halo(1, ybuf.at[0])
-    nacc[...] = near(1024, 2048)
     gram_own()
     far_partial(1)
+    nacc[...] = near(1024, 2048)
     plane_to_z(1)
     take_halo(1)
     nacc[...] += near(0, 1024) + near(2048, 3072)
@@ -464,9 +466,9 @@
     send_coeffs(2)
     send_halo(2, ybuf.at[1])
     nacc[...] = near(1024, 2048)
-    mix_send()
     plane_to_z(2)
     far_partial(2)
+    mix_send()
     take_halo(2)
     nacc[...] += near(0, 1024) + near(2048, 3072)
     z_to_x(2, gain * mix())

time: 82.1 us -> 83.2 us (1.013)
  Pallas kernels: 80.4 us -> 81.6 us
    pallas_call x1, Pallas kernels: 80.4 us -> 81.6 us  [on_device(): pl.pallas_call(kernel, out_shape=jax.ShapeDtypeStruct((16, 1024), F32), i...]
where the time goes in v4:
time: 83.2 us; the launch traced here: 83 us
  Pallas kernels  81.6 us (98%)
  local copies, waits for them, and re-layouts  1.47 us (2%)
    pallas_call x1, Pallas kernels, on_device(): pl.pallas_call(kernel, out_shape=jax.ShapeDtypeStruct((16, 1024), F32), i...  81.6 us

profile of v4, /device:TPU:1, one launch (start us, length us, event | category | flops | bytes accessed | tf_op | source)
XLA Modules:
  0.0 83.0 jit_solution(11127001728183372929)
XLA Ops:
  0.0 81.6 %filter.1 = f32[16,1024]{1,0:T(8,128)} custom-call(f32[16,1024]{1,0:T(8,128)} %vec_in.1, f32[3,1024]{1,0:T(4,128)} %pts_in.1, s32[2,6]{1,0:T(2,128)} %near_in.1, s32[2,16]{1,0:T(2,128)} %inter_in.1, s32[2,64]{1,0:T(2,128)} %skel_in.1, f32[2,64,512]{2,1,0:T(8,128)} %interp_in.1, f32[2,64,128]{2,1,0:T(8,128)} %trans_in.1, f32[3,8,128]{2,1,0:T(8,128)} %bitcast.1), custom_call_target="tpu_custom_call" | custom-call | tf_op jit(solution)/shard_map/filter/pallas_call | solution.py:515
  81.6 1.5 %copy.10 = f32[16,1024]{1,0:T(8,128)} copy(f32[16,1024]{1,0:T(8,128)} %filter.1) | data formatting | bytes 131072

commit v5 on v4

--- a/solution.py
+++ b/solution.py
@@ -431,8 +431,9 @@
     far_partial(0)
     arrived(xh, PTS)
     near_features(xh[0], 0)
-    near_kernel(0)
+    near_kernel(0, 0, 1)
     z_to_x(0)
+    near_kernel(0, 1, 2)
     near_features(xh[1], 4)
     near_kernel(2048)
     take_halo(0)
@@ -443,12 +444,12 @@
     gain = 2.0 / (HALF_WIDTH * SCALE)
     split_field(ybuf[0])
     upward(1)
+    send_plane(1)
     send_coeffs(1)
-    send_plane(1)
     send_halo(1, ybuf.at[0])
+    nacc[...] = near(1024, 2048)
     gram_own()
     far_partial(1)
-    nacc[...] = near(1024, 2048)
     plane_to_z(1)
     take_halo(1)
     nacc[...] += near(0, 1024) + near(2048, 3072)
@@ -466,9 +467,9 @@
     send_coeffs(2)
     send_halo(2, ybuf.at[1])
     nacc[...] = near(1024, 2048)
+    mix_send()
     plane_to_z(2)
     far_partial(2)
-    mix_send()
     take_halo(2)
     nacc[...] += near(0, 1024) + near(2048, 3072)
     z_to_x(2, gain * mix())

time: 83.2 us -> 83.2 us (level)
  no operation moved by 1% of the time
where the time goes in v5:
time: 83.2 us; the launch traced here: 83 us
  Pallas kernels  81.5 us (98%)
  local copies, waits for them, and re-layouts  1.47 us (2%)
    pallas_call x1, Pallas kernels, on_device(): pl.pallas_call(kernel, out_shape=jax.ShapeDtypeStruct((16, 1024), F32), i...  81.5 us

profile of v5, /device:TPU:1, one launch (start us, length us, event | category | flops | bytes accessed | tf_op | source)
XLA Modules:
  0.0 83.0 jit_solution(17201830749749588921)
XLA Ops:
  0.0 81.5 %filter.1 = f32[16,1024]{1,0:T(8,128)} custom-call(f32[16,1024]{1,0:T(8,128)} %vec_in.1, f32[3,1024]{1,0:T(4,128)} %pts_in.1, s32[2,6]{1,0:T(2,128)} %near_in.1, s32[2,16]{1,0:T(2,128)} %inter_in.1, s32[2,64]{1,0:T(2,128)} %skel_in.1, f32[2,64,512]{2,1,0:T(8,128)} %interp_in.1, f32[2,64,128]{2,1,0:T(8,128)} %trans_in.1, f32[3,8,128]{2,1,0:T(8,128)} %bitcast.1), custom_call_target="tpu_custom_call" | custom-call | tf_op jit(solution)/shard_map/filter/pallas_call | solution.py:516
  81.5 1.5 %copy.10 = f32[16,1024]{1,0:T(8,128)} copy(f32[16,1024]{1,0:T(8,128)} %filter.1) | data formatting | bytes 131072
